TPU v7x, 128 devices: a whole 4x4x4 slice. The times are simulated.
128 devices in a mesh: dp: 8 (over x, core), token: 16 (over z, y).
Axes of the slice: x: 4, y: 4, z: 4, core: 2. Of those that a mesh axis runs over, the one named last changes fastest.
Arguments:
- dense_tokens: bfloat16 [2048, 15, 768], P(('dp', 'token')), may hold values from -6 to 6
- cold_table: bfloat16 [131072, 128], P('dp'), may hold values from -6 to 6
- cold_ids: int32 [2048, 6, 16], P(('dp', 'token')), may hold values from 0 to 131071
- routes: int32 [16, 2048, 2], P(None, ('dp', 'token')), may hold values from 0 to 7, all different within a row; in each aligned block of 16 rows (0 to 15, 16 to 31, ..., all dimensions but the last counted through in order) at most 8 rows name the same one
- router: bfloat16 [16, 768, 8], replicated, may hold values from -0.21875 to 0.21875
- w_in: bfloat16 [16, 8, 768, 3072], P('token', 'dp'), may hold values from -0.21875 to 0.21875
- w_out: bfloat16 [16, 8, 3072, 768], P('token', 'dp'), may hold values from -0.109375 to 0.109375
Outputs:
- block_out: bfloat16 [2048, 16, 768], P(('dp', 'token'))
Inputs may be any that keep to these rules, and one draw needn't show every extreme that they name: `routes`: the two experts of a row differ. In each aligned block of 16 rows along the samples (one device's samples for one token) no expert is named by more than 8 rows.
All inputs are finite; a program needn't handle non-finite values.
Results may differ from a plain program's by a relative error of at most 0.01.
Values may be sent and summed in bfloat16 or wider, within the bound.
A program may use at most 64 MiB of HBM per device.

v0:
```python
import functools
import math

import jax
import jax.numpy as jnp
from jax import lax
from jax.experimental import pallas as pl
from jax.experimental.pallas import tpu as pltpu
from jax.sharding import PartitionSpec as P

CHUNKS = 4
PER = 32
CAP = 8
MESH = pl.DeviceIdType.MESH


def offsets(r):
    chunk, within = r // PER, r % PER
    dz, place = within // 8, within % 8
    return place // 2, place % 2, dz, (chunk + 4 - dz) % 4


def target_of(r, dp, tk):
    dx, dc, dz, dy = offsets(r)
    return (
        ((dp // 2 + dx) % 4) * 2 + (dp % 2 + dc) % 2,
        ((tk // 4 + dz) % 4) * 4 + (tk % 4 + dy) % 4,
    )


def source_of(r, dp, tk):
    dx, dc, dz, dy = offsets(r)
    return (
        ((dp // 2 + 4 - dx) % 4) * 2 + (dp % 2 + dc) % 2,
        ((tk // 4 + 4 - dz) % 4) * 4 + (tk % 4 + 4 - dy) % 4,
    )


def layer_norm(value):
    mean = jnp.mean(value, axis=-1, keepdims=True)
    centred = value - mean
    var = jnp.mean(centred * centred, axis=-1, keepdims=True)
    return centred * lax.rsqrt(var + 1e-05)


def gelu(value):
    return 0.5 * value * (1.0 + lax.erf(value * math.sqrt(0.5)))


def block_kernel(
    dense_ref, cold_ref, routes_ref, router_ref, w1_hbm, w2_hbm, out_ref,
    w1, w2, send, recv, back_send, back, slots, normed,
    w_sem, send_sem, recv_sem, back_send_sem, back_sem,
):
    dp, tk = lax.axis_index("dp"), lax.axis_index("token")
    mine = tk * 8 + dp
    load1 = pltpu.make_async_copy(w1_hbm, w1, w_sem.at[0])
    load2 = pltpu.make_async_copy(w2_hbm, w2, w_sem.at[1])
    load1.start()
    load2.start()
    barrier = pltpu.get_barrier_semaphore()

    def greet(r, carry):
        pl.semaphore_signal(barrier, inc=1, device_id=target_of(r, dp, tk), device_id_type=MESH)
        return carry

    lax.fori_loop(1, CHUNKS * PER, greet, 0)

    expert = lax.broadcasted_iota(jnp.int32, (16, 8, 32), 1)
    picks = (routes_ref[:, 0:1, :] == expert) | (routes_ref[:, 1:2, :] == expert)
    row = lax.broadcasted_iota(jnp.int32, (32, 32), 0)
    col = lax.broadcasted_iota(jnp.int32, (32, 32), 1)
    before = jnp.where((row // 16 == col // 16) & (row < col), 1.0, 0.0).astype(jnp.bfloat16)
    ones = jnp.where(picks, 1.0, 0.0)
    place = jnp.dot(
        ones.reshape(128, 32).astype(jnp.bfloat16), before, preferred_element_type=jnp.float32
    ).reshape(16, 8, 32)
    place = jnp.where(picks, place, -1.0)
    slot = lax.broadcasted_iota(jnp.int32, (16, 16, 32), 1)
    half = lax.broadcasted_iota(jnp.int32, (16, 16, 32), 2) // 16
    number = jnp.where(slot // 8 == half, slot % 8, -2).astype(jnp.float32)
    for e in range(8):
        slots[:, e * 16:(e + 1) * 16, :] = jnp.where(
            place[:, e:e + 1, :] == number, 1.0, 0.0
        ).astype(jnp.bfloat16)

    features = [dense_ref[t] for t in range(15)] + [cold_ref[...]]
    for h in range(16):
        mixed = jnp.concatenate([f[:, h * 48:(h + 1) * 48] for f in features], axis=1)
        rows = layer_norm(mixed.astype(jnp.float32) + features[h].astype(jnp.float32))
        rows = rows.astype(jnp.bfloat16)
        normed[h] = rows
        halves = jnp.concatenate([rows[:, :384], rows[:, 384:]], axis=0)
        out = jnp.dot(slots[h], halves, preferred_element_type=jnp.float32)
        send[h * 8:(h + 1) * 8] = out.astype(jnp.bfloat16).reshape(8, 16, 384)

    pl.semaphore_wait(barrier, CHUNKS * PER - 1)

    def post(r, carry):
        e, t = target_of(r, dp, tk)
        pltpu.make_async_remote_copy(
            src_ref=send.at[t * 8 + e], dst_ref=recv.at[r],
            send_sem=send_sem, recv_sem=recv_sem.at[r // PER],
            device_id=(e, t), device_id_type=MESH,
        ).start()
        return carry

    lax.fori_loop(1, CHUNKS * PER, post, 0)
    pltpu.make_async_copy(send.at[mine], recv.at[0], recv_sem.at[0]).start()
    load1.wait()
    load2.wait()
    which = lax.broadcasted_iota(jnp.int32, (PER * CAP, 8), 1) == dp

    def work(c, carry):
        span = pl.ds(c * PER, PER)
        pltpu.make_async_copy(recv.at[span], recv.at[span], recv_sem.at[c]).wait()
        got = recv[span].astype(jnp.float32)
        rows = jnp.concatenate([got[:, :CAP], got[:, CAP:]], axis=2)
        rows = rows.reshape(PER * CAP, 768).astype(jnp.bfloat16)
        total = jnp.zeros((PER * CAP, 768), jnp.float32)
        for j in range(4):
            hidden = jnp.dot(rows, w1[:, j * 768:(j + 1) * 768], preferred_element_type=jnp.float32)
            hidden = gelu(hidden).astype(jnp.bfloat16)
            total += jnp.dot(hidden, w2[j * 768:(j + 1) * 768, :], preferred_element_type=jnp.float32)
        logits = lax.dot_general(
            rows, router_ref[tk], (((1,), (1,)), ((), ())), preferred_element_type=jnp.float32
        )
        gate = jax.nn.sigmoid(jnp.sum(jnp.where(which, logits, 0.0), axis=1, keepdims=True))
        total = (total * gate).reshape(PER, CAP, 768)
        back_send[span] = jnp.concatenate(
            [total[:, :, :384], total[:, :, 384:]], axis=1
        ).astype(jnp.bfloat16)

        def reply(r, carry):
            e, t = source_of(r, dp, tk)
            pltpu.make_async_remote_copy(
                src_ref=back_send.at[r], dst_ref=back.at[mine],
                send_sem=back_send_sem, recv_sem=back_sem.at[c],
                device_id=(e, t), device_id_type=MESH,
            ).start()
            return carry

        lax.fori_loop(jnp.where(c == 0, 1, c * PER), (c + 1) * PER, reply, 0)

        @pl.when(c == 0)
        def _():
            pltpu.make_async_copy(back_send.at[0], back.at[mine], back_sem.at[0]).start()

        return carry

    lax.fori_loop(0, CHUNKS, work, 0)

    def finish(c, carry):
        span = pl.ds(c * PER, PER)
        pltpu.make_async_copy(back.at[span], back.at[span], back_sem.at[c]).wait()
        for q in range(4):
            t = ((tk // 4 + q) % 4) * 4 + (tk % 4 + c + 4 - q) % 4
            answers = back[pl.ds(t * 8, 8)].reshape(128, 384)
            moe = lax.dot_general(
                slots[t], answers, (((0,), (0,)), ((), ())), preferred_element_type=jnp.float32
            )
            moe = jnp.concatenate([moe[:16], moe[16:]], axis=1)
            out_ref[t] = layer_norm(normed[t].astype(jnp.float32) + moe).astype(jnp.bfloat16)
        return carry

    lax.fori_loop(0, CHUNKS, finish, 0)
    sent = pl.ds(1, CHUNKS * PER - 1)
    pltpu.make_async_copy(send.at[sent], send.at[sent], send_sem).wait()
    pltpu.make_async_copy(back_send.at[sent], back_send.at[sent], back_send_sem).wait()


def run_block(dense, cold, routes, router, w_in, w_out):
    vmem = pl.BlockSpec(memory_space=pltpu.VMEM)
    return pl.pallas_call(
        block_kernel,
        out_shape=jax.ShapeDtypeStruct((16, 16, 768), jnp.bfloat16),
        in_specs=[vmem] * 4 + [pl.BlockSpec(memory_space=pl.ANY)] * 2,
        out_specs=vmem,
        scratch_shapes=[
            pltpu.VMEM((768, 3072), jnp.bfloat16),
            pltpu.VMEM((3072, 768), jnp.bfloat16),
        ]
        + [pltpu.VMEM((128, 16, 384), jnp.bfloat16)] * 4
        + [
            pltpu.VMEM((16, 128, 32), jnp.bfloat16),
            pltpu.VMEM((16, 16, 768), jnp.bfloat16),
            pltpu.SemaphoreType.DMA((2,)),
            pltpu.SemaphoreType.DMA,
            pltpu.SemaphoreType.DMA((CHUNKS,)),
            pltpu.SemaphoreType.DMA,
            pltpu.SemaphoreType.DMA((CHUNKS,)),
        ],
        compiler_params=pltpu.CompilerParams(
            collective_id=0, has_side_effects=True, vmem_limit_bytes=48 * 1024 * 1024
        ),
        cost_estimate=pl.CostEstimate(
            flops=4 * 1024 * 768 * 3072, bytes_accessed=2 * 2 * 768 * 3072, transcendentals=0
        ),
    )(dense, cold, routes, router, w_in, w_out)


def shards(dense_tokens, cold_table, cold_ids, routes, router, w_in, w_out):
    samples = dense_tokens.shape[0]
    emb_width = cold_table.shape[1]
    rows_own = cold_table.shape[0]
    lists = cold_ids.shape[1]
    length = cold_ids.shape[2]
    gathered_ids = lax.all_gather(cold_ids, "dp", axis=0, tiled=True)
    base = lax.axis_index("dp") * rows_own
    factor = 1.0 / math.sqrt(length)
    local = gathered_ids - base
    inside = ((local >= 0) & (local < rows_own)).astype(jnp.bfloat16)
    found = jnp.take(cold_table, jnp.clip(local, 0, rows_own - 1), axis=0)
    summed = jnp.einsum("bgl,bgle->bge", inside, found, preferred_element_type=jnp.float32)
    cold = lax.psum_scatter(
        (summed.reshape(samples * lax.axis_size("dp"), lists * emb_width) * factor).astype(
            jnp.bfloat16
        ),
        "dp",
        scatter_dimension=0,
        tiled=True,
    )
    routes = routes.transpose(0, 2, 1)
    out = run_block(
        dense_tokens.transpose(1, 0, 2),
        cold,
        jnp.concatenate([routes, routes], axis=2),
        router.transpose(0, 2, 1),
        w_in[0, 0],
        w_out[0, 0],
    )
    return out.transpose(1, 0, 2)


def solution(mesh):
    return jax.shard_map(
        shards,
        mesh=mesh,
        in_specs=(
            P(("dp", "token"), None, None),
            P("dp", None),
            P(("dp", "token"), None, None),
            P(None, ("dp", "token"), None),
            P(),
            P("token", "dp", None, None),
            P("token", "dp", None, None),
        ),
        out_specs=P(("dp", "token"), None, None),
        check_vma=False,
    )
```

profile of v0, /device:TPU:1, one launch (start us, length us, event | category | flops | bytes accessed | tf_op | source)
XLA Modules:
  0.0 171.0 jit_solution(15196403495274177604)
XLA Ops:
  6.5 0.0 reduce-scatter.2.cloned.1.call-start
  6.5 0.8 copy.19
  7.4 14.8 %all_gather.3 = s32[128,6,16]{2,1,0:T(8,128)S(1)} all-gather(s32[16,6,16]{2,1,0:T(8,128)S(1)} %copy.19), channel_id=1, replica_groups=mesh['dp'=8,'token'=16] {'dp'}, dimensions={0}, use_global_device_ids=true | all-gather | bytes 55296 | tf_op jit(solution)/shard_map/all_gather | solution.py:208
  22.2 0.2 copy.20
  22.3 0.1 compare_and_fusion
  22.4 0.2 copy.22
  22.6 0.2 reshape.11
  22.8 0.2 copy.30
  23.0 0.3 copy.21
  23.3 44.2 %gather_fusion = bf16[12288,128]{1,0:T(8,128)(2,1)} fusion(bf16[16384,128]{1,0:T(8,128)(2,1)} %param.8, s32[12288]{0:T(1024)S(1)} %broadcast_clamp_fusion), kind=kCustom, calls=%fused_computation | custom fusion | bytes 6340608 | tf_op jit(solution)/shard_map/jit(_take)/gather | solution.py:213
  67.5 0.0 copy-start.4
  67.5 0.0 copy-start.1
  67.5 0.0 copy-start.2
  67.5 8.6 %multiply_reduce_fusion = f32[128,6,128]{2,1,0:T(8,128)S(1)} fusion(f32[128,6,16]{2,1,0:T(8,128)S(1)} %copy.30, bf16[128,6,16,128]{3,2,1,0:T(8,128)(2,1)} %bitcast.12, pred[128,6,16]{2,1,0:T(8,128)(4,1)S(1)} %copy.21), kind=kLoop, calls=%fused_computation.1 | loop fusion | flops 6193152 | bytes 3600384
  76.1 0.2 copy.29
  76.4 0.8 copy.23
  77.2 0.0 reduce-scatter.2.cloned.1.call-update
  77.2 0.0 copy-done.4
  77.2 0.1 pad_add_fusion.routes_ref
  77.3 29.0 %reduce-scatter.2.cloned.1.call-done.cold_ref = bf16[16,768]{1,0:T(8,128)(2,1)} async-done(((bf16[128,768]{1,0:T(8,128)(2,1)}), bf16[16,768]{1,0:T(8,128)(2,1)}) %reduce-scatter.2.cloned.1.call-update) | async-done | bytes 24592 | tf_op jit(solution)/shard_map/reduce_scatter | solution.py:215
  106.3 0.0 copy-done.1
  106.3 0.0 copy-done.2
  106.3 0.0 copy-start
  106.3 2.3 %copy-done = bf16[1,1,768,3072]{3,2,1,0:T(8,128)(2,1)S(1)} copy-done((bf16[1,1,768,3072]{3,2,1,0:T(8,128)(2,1)S(1)}, bf16[1,1,768,3072]{3,2,1,0:T(8,128)(2,1)}, u32[]{:S(2)}) %copy-start) | copy-done | bytes 4718616
  108.7 0.0 copy-start.3
  108.7 0.7 copy-done.3
  109.4 53.8 %shard_map.73 = bf16[16,16,768]{2,1,0:T(8,128)(2,1)S(1)} custom-call(bf16[15,16,768]{2,1,0:T(8,128)(2,1)S(1)} %bitcast.10, bf16[16,768]{1,0:T(8,128)(2,1)S(1)} %copy-done.3, s32[16,2,32]{2,1,0:T(2,128)S(1)} %pad_add_fusion.routes_ref, bf16[16,8,768]{2,1,0:T(8,128)(2,1)S(1)} %bitcast.11, bf16[768,3072]{1,0:T(8,128)(2,1)S(1)} %bitcast.9, ...), custom_call_target="tpu_custom_call" | custom-call | flops 9663676416 | bytes 9437184 | tf_op jit(solution)/shard_map/pallas_call | solution.py:174
  163.3 0.9 copy.24
  (2 shorter events, 0.0 us)
Async XLA Ops:
  6.5 99.8 %reduce-scatter.2.cloned.1.call-start = ((), (), s32[]{:S(2)}) async-start(), calls=%async_computation.1 | async-start | bytes 221184 | tf_op jit(solution)/shard_map/reduce_scatter | solution.py:215
  67.5 9.7 %copy-start.4 = (s32[16,16,2]{1,2,0:T(2,128)S(1)}, s32[16,16,2]{1,2,0:T(2,128)}, u32[]{:S(2)}) copy-start(s32[16,16,2]{1,2,0:T(2,128)} %param.10) | copy-start | bytes 6148
  67.5 38.8 %copy-start.1 = (bf16[16,15,768]{2,0,1:T(8,128)(2,1)S(1)}, bf16[16,15,768]{2,0,1:T(8,128)(2,1)}, u32[]{:S(2)}) copy-start(bf16[16,15,768]{2,0,1:T(8,128)(2,1)} %param.7) | copy-start | bytes 1105924
  67.5 38.8 %copy-start.2 = (bf16[16,768,8]{1,2,0:T(8,128)(2,1)S(1)}, bf16[16,768,8]{1,2,0:T(8,128)(2,1)}, u32[]{:S(2)}) copy-start(bf16[16,768,8]{1,2,0:T(8,128)(2,1)} %param.11) | copy-start | bytes 589828
  106.3 2.3 %copy-start = (bf16[1,1,768,3072]{3,2,1,0:T(8,128)(2,1)S(1)}, bf16[1,1,768,3072]{3,2,1,0:T(8,128)(2,1)}, u32[]{:S(2)}) copy-start(bf16[1,1,768,3072]{3,2,1,0:T(8,128)(2,1)} %param.12) | copy-start | bytes 14155780
  108.7 0.7 copy-start.3
Sparse Core Ops, SparseCore 0:
  77.3 28.9 reduce-scatter.1
where the time goes:
time: 173 us; the launch traced here: 171 us
  Pallas kernels  53.8 us (31%)
  local copies, waits for them, and re-layouts  51 us (29%)
  waiting for transfers between devices  29 us (17%)
  blocking collectives  14.8 us (9%)
  between operations  13.5 us (8%)
  other arithmetic  8.81 us (5%)
    pallas_call x1, Pallas kernels, run_block(): pl.pallas_call(block_kernel, out_shape=jax.ShapeDtypeStruct((16, 16, 768)...  53.8 us
    gather x1, local copies, waits for them, and re-layouts, shards(): found = jnp.take(cold_table, jnp.clip(local, 0, rows_own - 1), axis=0)  44.2 us
    reduce_scatter x1, waiting for transfers between devices, shards(): lax.psum_scatter((summed.reshape(samples * lax.axis_size('dp'), lists * e...  29 us
    all_gather x1, blocking collectives, shards(): gathered_ids = lax.all_gather(cold_ids, 'dp', axis=0, tiled=True)  14.8 us
    unnamed x1, other arithmetic  8.63 us
    unnamed x12, local copies, waits for them, and re-layouts  4.14 us
  transfers between devices with their start and end apart: 1, of which 1 were waited for; matrix products, arithmetic and copies ran while one was open for 0% of the time, Pallas kernels for 0%

commit v1 on v0

--- a/solution.py
+++ b/solution.py
@@ -36,6 +36,10 @@
     )
 
 
+def peer_of(k, dp, way):
+    return ((dp // 2 + 4 + way * (k // 2)) % 4) * 2 + (dp % 2 + k) % 2
+
+
 def layer_norm(value):
     mean = jnp.mean(value, axis=-1, keepdims=True)
     centred = value - mean
@@ -48,12 +52,15 @@
 
 
 def block_kernel(
-    dense_ref, cold_ref, routes_ref, router_ref, w1_hbm, w2_hbm, out_ref,
+    dense_ref, ids_ref, routes_ref, router_ref, table_hbm, w1_hbm, w2_hbm, out_ref,
     w1, w2, send, recv, back_send, back, slots, normed,
-    w_sem, send_sem, recv_sem, back_send_sem, back_sem,
+    table, ids, counts, sums, part_send, part,
+    w_sem, send_sem, recv_sem, back_send_sem, back_sem, id_send_sem, id_sem, part_send_sem, part_sem,
 ):
     dp, tk = lax.axis_index("dp"), lax.axis_index("token")
     mine = tk * 8 + dp
+    load_table = pltpu.make_async_copy(table_hbm, table, w_sem.at[2])
+    load_table.start()
     load1 = pltpu.make_async_copy(w1_hbm, w1, w_sem.at[0])
     load2 = pltpu.make_async_copy(w2_hbm, w2, w_sem.at[1])
     load1.start()
@@ -84,7 +91,73 @@
             place[:, e:e + 1, :] == number, 1.0, 0.0
         ).astype(jnp.bfloat16)
 
-    features = [dense_ref[t] for t in range(15)] + [cold_ref[...]]
+    pl.semaphore_wait(barrier, CHUNKS * PER - 1)
+    for k in range(1, 8):
+        pltpu.make_async_remote_copy(
+            src_ref=ids_ref, dst_ref=ids.at[k], send_sem=id_send_sem.at[k - 1],
+            recv_sem=id_sem.at[k - 1], device_id=(peer_of(k, dp, 1), tk), device_id_type=MESH,
+        ).start()
+    ids[0] = ids_ref[...]
+    load_table.wait()
+    own_rows = table.shape[0]
+    diagonal = (
+        lax.broadcasted_iota(jnp.int32, (16, 256), 0)
+        == lax.broadcasted_iota(jnp.int32, (16, 256), 1) // 16
+    )
+    low_row = lax.broadcasted_iota(jnp.int32, (256, 256), 0).astype(jnp.float32).astype(jnp.bfloat16)
+    one, none = jnp.ones((), jnp.bfloat16), jnp.zeros((), jnp.bfloat16)
+    for part_no in range(2):
+        for k in range(part_no * 4, part_no * 4 + 4):
+            if k:
+                pltpu.make_async_copy(ids.at[k], ids.at[k], id_sem.at[k - 1]).wait()
+
+        def count(group, carry):
+            local = ids[part_no * 4 + group // 6, pl.ds(group % 6, 1), :] - dp * own_rows
+            inside = (local >= 0) & (local < own_rows)
+            high = jnp.where(inside & diagonal, local // 256, -1)
+            high = high.astype(jnp.float32).astype(jnp.bfloat16)
+            low = jnp.where(inside, local % 256, 0).astype(jnp.float32).astype(jnp.bfloat16)
+            lefts = jnp.concatenate(
+                [jnp.where(high == float(i), one, none) for i in range(own_rows // 256)], axis=0
+            )
+            right = jnp.where(low_row == low, one, none)
+            found = lax.dot_general(
+                lefts, right, (((1,), (1,)), ((), ())), preferred_element_type=jnp.float32
+            ).astype(jnp.bfloat16)
+            rows = pl.ds(pl.multiple_of(group * 16, 16), 16)
+            for i in range(own_rows // 256):
+                counts[rows, i * 256:(i + 1) * 256] = found[i * 16:(i + 1) * 16]
+            return carry
+
+        lax.fori_loop(0, 24, count, 0)
+        sums[...] = jnp.zeros_like(sums)
+
+        def pool(step, carry):
+            at = pl.ds(pl.multiple_of(step * 2048, 2048), 2048)
+            sums[...] += jnp.dot(counts[:, at], table[at, :], preferred_element_type=jnp.float32)
+            return carry
+
+        lax.fori_loop(0, own_rows // 2048, pool, 0)
+        pooled = (sums[...] * 0.25).astype(jnp.bfloat16).reshape(4, 96, 128)
+        for k in range(part_no * 4, part_no * 4 + 4):
+            if k == 0:
+                part[0] = pooled[0]
+            else:
+                part_send[k] = pooled[k % 4]
+                pltpu.make_async_remote_copy(
+                    src_ref=part_send.at[k], dst_ref=part.at[k], send_sem=part_send_sem.at[k - 1],
+                    recv_sem=part_sem.at[k - 1], device_id=(peer_of(k, dp, -1), tk),
+                    device_id_type=MESH,
+                ).start()
+    for k in range(1, 8):
+        pltpu.make_async_copy(part.at[k], part.at[k], part_sem.at[k - 1]).wait()
+    cold = part[0].astype(jnp.float32)
+    for k in range(1, 8):
+        cold += part[k].astype(jnp.float32)
+    cold = cold.astype(jnp.bfloat16)
+    cold = jnp.concatenate([cold[g * 16:(g + 1) * 16] for g in range(6)], axis=1)
+
+    features = [dense_ref[t] for t in range(15)] + [cold]
     for h in range(16):
         mixed = jnp.concatenate([f[:, h * 48:(h + 1) * 48] for f in features], axis=1)
         rows = layer_norm(mixed.astype(jnp.float32) + features[h].astype(jnp.float32))
@@ -93,8 +166,6 @@
         halves = jnp.concatenate([rows[:, :384], rows[:, 384:]], axis=0)
         out = jnp.dot(slots[h], halves, preferred_element_type=jnp.float32)
         send[h * 8:(h + 1) * 8] = out.astype(jnp.bfloat16).reshape(8, 16, 384)
-
-    pl.semaphore_wait(barrier, CHUNKS * PER - 1)
 
     def post(r, carry):
         e, t = target_of(r, dp, tk)
@@ -164,17 +235,20 @@
         return carry
 
     lax.fori_loop(0, CHUNKS, finish, 0)
+    for k in range(1, 8):
+        pltpu.make_async_copy(ids_ref, ids_ref, id_send_sem.at[k - 1]).wait()
+        pltpu.make_async_copy(part_send.at[k], part_send.at[k], part_send_sem.at[k - 1]).wait()
     sent = pl.ds(1, CHUNKS * PER - 1)
     pltpu.make_async_copy(send.at[sent], send.at[sent], send_sem).wait()
     pltpu.make_async_copy(back_send.at[sent], back_send.at[sent], back_send_sem).wait()
 
 
-def run_block(dense, cold, routes, router, w_in, w_out):
+def run_block(dense, ids, routes, router, table, w_in, w_out):
     vmem = pl.BlockSpec(memory_space=pltpu.VMEM)
     return pl.pallas_call(
         block_kernel,
         out_shape=jax.ShapeDtypeStruct((16, 16, 768), jnp.bfloat16),
-        in_specs=[vmem] * 4 + [pl.BlockSpec(memory_space=pl.ANY)] * 2,
+        in_specs=[vmem] * 4 + [pl.BlockSpec(memory_space=pl.ANY)] * 3,
         out_specs=vmem,
         scratch_shapes=[
             pltpu.VMEM((768, 3072), jnp.bfloat16),
@@ -184,48 +258,38 @@
         + [
             pltpu.VMEM((16, 128, 32), jnp.bfloat16),
             pltpu.VMEM((16, 16, 768), jnp.bfloat16),
-            pltpu.SemaphoreType.DMA((2,)),
+            pltpu.VMEM(table.shape, jnp.bfloat16),
+            pltpu.VMEM((8, 8, 256), jnp.int32),
+            pltpu.VMEM((384, table.shape[0]), jnp.bfloat16),
+            pltpu.VMEM((384, 128), jnp.float32),
+            pltpu.VMEM((8, 96, 128), jnp.bfloat16),
+            pltpu.VMEM((8, 96, 128), jnp.bfloat16),
+            pltpu.SemaphoreType.DMA((3,)),
             pltpu.SemaphoreType.DMA,
             pltpu.SemaphoreType.DMA((CHUNKS,)),
             pltpu.SemaphoreType.DMA,
             pltpu.SemaphoreType.DMA((CHUNKS,)),
-        ],
+        ]
+        + [pltpu.SemaphoreType.DMA((7,))] * 4,
         compiler_params=pltpu.CompilerParams(
-            collective_id=0, has_side_effects=True, vmem_limit_bytes=48 * 1024 * 1024
+            collective_id=0, has_side_effects=True, vmem_limit_bytes=58 * 1024 * 1024
         ),
         cost_estimate=pl.CostEstimate(
             flops=4 * 1024 * 768 * 3072, bytes_accessed=2 * 2 * 768 * 3072, transcendentals=0
         ),
-    )(dense, cold, routes, router, w_in, w_out)
+    )(dense, ids, routes, router, table, w_in, w_out)
 
 
 def shards(dense_tokens, cold_table, cold_ids, routes, router, w_in, w_out):
-    samples = dense_tokens.shape[0]
-    emb_width = cold_table.shape[1]
-    rows_own = cold_table.shape[0]
-    lists = cold_ids.shape[1]
-    length = cold_ids.shape[2]
-    gathered_ids = lax.all_gather(cold_ids, "dp", axis=0, tiled=True)
-    base = lax.axis_index("dp") * rows_own
-    factor = 1.0 / math.sqrt(length)
-    local = gathered_ids - base
-    inside = ((local >= 0) & (local < rows_own)).astype(jnp.bfloat16)
-    found = jnp.take(cold_table, jnp.clip(local, 0, rows_own - 1), axis=0)
-    summed = jnp.einsum("bgl,bgle->bge", inside, found, preferred_element_type=jnp.float32)
-    cold = lax.psum_scatter(
-        (summed.reshape(samples * lax.axis_size("dp"), lists * emb_width) * factor).astype(
-            jnp.bfloat16
-        ),
-        "dp",
-        scatter_dimension=0,
-        tiled=True,
-    )
+    ids = cold_ids.transpose(1, 0, 2).reshape(6, 256)
+    ids = jnp.concatenate([ids, ids[:2]], axis=0)
     routes = routes.transpose(0, 2, 1)
     out = run_block(
         dense_tokens.transpose(1, 0, 2),
-        cold,
+        ids,
         jnp.concatenate([routes, routes], axis=2),
         router.transpose(0, 2, 1),
+        cold_table,
         w_in[0, 0],
         w_out[0, 0],
     )

time: 173 us -> 98.1 us (0.57)
  local copies, waits for them, and re-layouts: 51 us -> 3.55 us
  Pallas kernels: 53.8 us -> 90.6 us
  waiting for transfers between devices: 29 us -> 0 us
  blocking collectives: 14.8 us -> 0 us
  between operations: 13.5 us -> 0.01 us
  other arithmetic: 8.81 us -> 2.09 us
    gather x1 -> x0, local copies, waits for them, and re-layouts: 44.2 us -> none  [shards(): found = jnp.take(cold_table, jnp.clip(local, 0, rows_own - 1), axis=0)]
    pallas_call x1, Pallas kernels: 53.8 us -> 90.6 us  [run_block(): pl.pallas_call(block_kernel, out_shape=jax.ShapeDtypeStruct((16, 16, 768)...]
    reduce_scatter x1 -> x0, waiting for transfers between devices: 29 us -> none  [shards(): lax.psum_scatter((summed.reshape(samples * lax.axis_size('dp'), lists * e...]
    all_gather x1 -> x0, blocking collectives: 14.8 us -> none  [shards(): gathered_ids = lax.all_gather(cold_ids, 'dp', axis=0, tiled=True)]
    unnamed x1 -> x0, other arithmetic: 8.63 us -> none
    unnamed x12 -> x0, local copies, waits for them, and re-layouts: 4.14 us -> none
  transfers between devices with their start and end apart: 1 -> 0, of which waited for: 1 -> 0; matrix products, arithmetic and copies ran while one was open for 0% -> 0% of each run, Pallas kernels for 0% -> 0%
where the time goes in v1:
time: 98.1 us; the launch traced here: 96.3 us
  Pallas kernels  90.6 us (92%)
  local copies, waits for them, and re-layouts  3.55 us (4%)
  other arithmetic  2.09 us (2%)
    pallas_call x1, Pallas kernels, run_block(): pl.pallas_call(block_kernel, out_shape=jax.ShapeDtypeStruct((16, 16, 768)...  90.6 us

profile of v1, /device:TPU:1, one launch (start us, length us, event | category | flops | bytes accessed | tf_op | source)
XLA Modules:
  0.0 96.3 jit_solution(11032800854287016173)
XLA Ops:
  0.0 0.9 reshape.4
  0.9 0.7 slice.8
  1.6 0.1 slice.7
  1.7 0.6 pad_add_fusion.1.ids_ref
  2.3 1.5 %pad_add_fusion.routes_ref = s32[16,2,32]{2,1,0:T(2,128)} fusion(s32[16,2,16]{2,1,0:T(2,128)} %bitcast.10), kind=kLoop, calls=%fused_computation | loop fusion | flops 1024 | bytes 6144 | tf_op jit(solution)/shard_map/concatenate | solution.py:290
  3.8 90.6 %shard_map.73 = bf16[16,16,768]{2,1,0:T(8,128)(2,1)} custom-call(bf16[15,16,768]{2,1,0:T(8,128)(2,1)} %bitcast.13, s32[8,256]{1,0:T(8,128)} %pad_add_fusion.1.ids_ref, s32[16,2,32]{2,1,0:T(2,128)} %pad_add_fusion.routes_ref, bf16[16,8,768]{2,1,0:T(8,128)(2,1)} %bitcast.14, bf16[16384,128]{1,0:T(8,128)(2,1)} %table_hbm.1, bf16[768,3072]{1,0:T(8,128)(2,1)} %bitcast.11, ...), custom_call_target="tpu_custom_call" | custom-call | flops 9663676416 | bytes 9437184 | tf_op jit(solution)/shard_map/pallas_call | solution.py:248
  94.4 1.9 %copy.8 = bf16[16,16,768]{2,1,0:T(8,128)(2,1)} copy(bf16[16,16,768]{2,0,1:T(8,128)(2,1)} %bitcast.7) | data formatting | bytes 786432 | tf_op jit(solution)/shard_map/transpose | solution.py:296

commit v2 on v1

--- a/solution.py
+++ b/solution.py
@@ -14,28 +14,6 @@
 MESH = pl.DeviceIdType.MESH
 
 
-def offsets(r):
-    chunk, within = r // PER, r % PER
-    dz, place = within // 8, within % 8
-    return place // 2, place % 2, dz, (chunk + 4 - dz) % 4
-
-
-def target_of(r, dp, tk):
-    dx, dc, dz, dy = offsets(r)
-    return (
-        ((dp // 2 + dx) % 4) * 2 + (dp % 2 + dc) % 2,
-        ((tk // 4 + dz) % 4) * 4 + (tk % 4 + dy) % 4,
-    )
-
-
-def source_of(r, dp, tk):
-    dx, dc, dz, dy = offsets(r)
-    return (
-        ((dp // 2 + 4 - dx) % 4) * 2 + (dp % 2 + dc) % 2,
-        ((tk // 4 + 4 - dz) % 4) * 4 + (tk % 4 + 4 - dy) % 4,
-    )
-
-
 def peer_of(k, dp, way):
     return ((dp // 2 + 4 + way * (k // 2)) % 4) * 2 + (dp % 2 + k) % 2
 
@@ -54,7 +32,7 @@
 def block_kernel(
     dense_ref, ids_ref, routes_ref, router_ref, table_hbm, w1_hbm, w2_hbm, out_ref,
     w1, w2, send, recv, back_send, back, slots, normed,
-    table, ids, counts, sums, part_send, part,
+    table, own_ids, ids, counts, sums, part_send, part,
     w_sem, send_sem, recv_sem, back_send_sem, back_sem, id_send_sem, id_sem, part_send_sem, part_sem,
 ):
     dp, tk = lax.axis_index("dp"), lax.axis_index("token")
@@ -65,16 +43,37 @@
     load2 = pltpu.make_async_copy(w2_hbm, w2, w_sem.at[1])
     load1.start()
     load2.start()
+    diagonal = (
+        lax.broadcasted_iota(jnp.int32, (16, 256), 0)
+        == lax.broadcasted_iota(jnp.int32, (16, 256), 1) // 16
+    )
     barrier = pltpu.get_barrier_semaphore()
 
-    def greet(r, carry):
-        pl.semaphore_signal(barrier, inc=1, device_id=target_of(r, dp, tk), device_id_type=MESH)
-        return carry
-
-    lax.fori_loop(1, CHUNKS * PER, greet, 0)
-
+    x, core, z, y = dp // 2, dp % 2, tk // 4, tk % 4
+    zs, ys = [(z + i) % 4 for i in range(4)], [(y + i) % 4 for i in range(4)]
+    experts = [((x + p // 2) % 4) * 2 + (core + p) % 2 for p in range(8)]
+    givers = [experts[(8 - p // 2 * 2) % 8 + p % 2] for p in range(8)]
+
+    def tokens(chunk, way):
+        return [
+            zs[way * q % 4] * 4 + (y + 4 + way * (chunk + 4 - q)) % 4
+            if not isinstance(chunk, int) else zs[way * q % 4] * 4 + ys[way * (chunk - q) % 4]
+            for q in range(4)
+        ]
+
+    for chunk in range(CHUNKS):
+        for q, t in enumerate(tokens(chunk, 1)):
+            for p, e in enumerate(experts):
+                if chunk + q + p:
+                    pl.semaphore_signal(barrier, inc=1, device_id=(e, t), device_id_type=MESH)
+
+    for g in range(6):
+        wide = jnp.concatenate([ids_ref[g]] * 16, axis=1)
+        own_ids[g:g + 1, :] = jnp.sum(jnp.where(diagonal, wide, 0), axis=0, keepdims=True)
+    own_ids[6:8, :] = jnp.zeros((2, 256), jnp.int32)
+    own_routes = jnp.concatenate([routes_ref[...]] * 2, axis=2)
     expert = lax.broadcasted_iota(jnp.int32, (16, 8, 32), 1)
-    picks = (routes_ref[:, 0:1, :] == expert) | (routes_ref[:, 1:2, :] == expert)
+    picks = (own_routes[:, 0:1, :] == expert) | (own_routes[:, 1:2, :] == expert)
     row = lax.broadcasted_iota(jnp.int32, (32, 32), 0)
     col = lax.broadcasted_iota(jnp.int32, (32, 32), 1)
     before = jnp.where((row // 16 == col // 16) & (row < col), 1.0, 0.0).astype(jnp.bfloat16)
@@ -94,16 +93,12 @@
     pl.semaphore_wait(barrier, CHUNKS * PER - 1)
     for k in range(1, 8):
         pltpu.make_async_remote_copy(
-            src_ref=ids_ref, dst_ref=ids.at[k], send_sem=id_send_sem.at[k - 1],
+            src_ref=own_ids, dst_ref=ids.at[k], send_sem=id_send_sem.at[k - 1],
             recv_sem=id_sem.at[k - 1], device_id=(peer_of(k, dp, 1), tk), device_id_type=MESH,
         ).start()
-    ids[0] = ids_ref[...]
+    ids[0] = own_ids[...]
     load_table.wait()
     own_rows = table.shape[0]
-    diagonal = (
-        lax.broadcasted_iota(jnp.int32, (16, 256), 0)
-        == lax.broadcasted_iota(jnp.int32, (16, 256), 1) // 16
-    )
     low_row = lax.broadcasted_iota(jnp.int32, (256, 256), 0).astype(jnp.float32).astype(jnp.bfloat16)
     one, none = jnp.ones((), jnp.bfloat16), jnp.zeros((), jnp.bfloat16)
     for part_no in range(2):
@@ -111,33 +106,37 @@
             if k:
                 pltpu.make_async_copy(ids.at[k], ids.at[k], id_sem.at[k - 1]).wait()
 
-        def count(group, carry):
-            local = ids[part_no * 4 + group // 6, pl.ds(group % 6, 1), :] - dp * own_rows
-            inside = (local >= 0) & (local < own_rows)
-            high = jnp.where(inside & diagonal, local // 256, -1)
-            high = high.astype(jnp.float32).astype(jnp.bfloat16)
-            low = jnp.where(inside, local % 256, 0).astype(jnp.float32).astype(jnp.bfloat16)
-            lefts = jnp.concatenate(
-                [jnp.where(high == float(i), one, none) for i in range(own_rows // 256)], axis=0
-            )
-            right = jnp.where(low_row == low, one, none)
-            found = lax.dot_general(
-                lefts, right, (((1,), (1,)), ((), ())), preferred_element_type=jnp.float32
-            ).astype(jnp.bfloat16)
-            rows = pl.ds(pl.multiple_of(group * 16, 16), 16)
-            for i in range(own_rows // 256):
-                counts[rows, i * 256:(i + 1) * 256] = found[i * 16:(i + 1) * 16]
+        def count(step, carry):
+            for u in range(6):
+                group = step * 6 + u
+                local = ids[part_no * 4 + group // 6, pl.ds(group % 6, 1), :] - dp * own_rows
+                inside = (local >= 0) & (local < own_rows)
+                high = jnp.where(inside & diagonal, local // 256, -1)
+                high = high.astype(jnp.float32).astype(jnp.bfloat16)
+                low = jnp.where(inside, local % 256, 0).astype(jnp.float32).astype(jnp.bfloat16)
+                right = jnp.where(low_row == low, one, none)
+                rows = pl.ds(pl.multiple_of(group * 16, 16), 16)
+                for v in range(4):
+                    lefts = jnp.concatenate(
+                        [jnp.where(high == float(v * 16 + i), one, none) for i in range(16)], axis=0
+                    )
+                    found = lax.dot_general(
+                        lefts, right, (((1,), (1,)), ((), ())), preferred_element_type=jnp.float32
+                    ).astype(jnp.bfloat16)
+                    for i in range(16):
+                        at = (v * 16 + i) * 256
+                        counts[rows, at:at + 256] = found[i * 16:(i + 1) * 16]
             return carry
 
-        lax.fori_loop(0, 24, count, 0)
+        lax.fori_loop(0, 24 // 6, count, 0)
         sums[...] = jnp.zeros_like(sums)
 
         def pool(step, carry):
-            at = pl.ds(pl.multiple_of(step * 2048, 2048), 2048)
+            at = pl.ds(pl.multiple_of(step * 8192, 8192), 8192)
             sums[...] += jnp.dot(counts[:, at], table[at, :], preferred_element_type=jnp.float32)
             return carry
 
-        lax.fori_loop(0, own_rows // 2048, pool, 0)
+        lax.fori_loop(0, own_rows // 8192, pool, 0)
         pooled = (sums[...] * 0.25).astype(jnp.bfloat16).reshape(4, 96, 128)
         for k in range(part_no * 4, part_no * 4 + 4):
             if k == 0:
@@ -167,16 +166,16 @@
         out = jnp.dot(slots[h], halves, preferred_element_type=jnp.float32)
         send[h * 8:(h + 1) * 8] = out.astype(jnp.bfloat16).reshape(8, 16, 384)
 
-    def post(r, carry):
-        e, t = target_of(r, dp, tk)
-        pltpu.make_async_remote_copy(
-            src_ref=send.at[t * 8 + e], dst_ref=recv.at[r],
-            send_sem=send_sem, recv_sem=recv_sem.at[r // PER],
-            device_id=(e, t), device_id_type=MESH,
-        ).start()
-        return carry
-
-    lax.fori_loop(1, CHUNKS * PER, post, 0)
+    for chunk in range(CHUNKS):
+        for q, t in enumerate(tokens(chunk, 1)):
+            for p, e in enumerate(experts):
+                r = chunk * PER + q * 8 + p
+                if r:
+                    pltpu.make_async_remote_copy(
+                        src_ref=send.at[t * 8 + e], dst_ref=recv.at[r],
+                        send_sem=send_sem, recv_sem=recv_sem.at[chunk],
+                        device_id=(e, t), device_id_type=MESH,
+                    ).start()
     pltpu.make_async_copy(send.at[mine], recv.at[0], recv_sem.at[0]).start()
     load1.wait()
     load2.wait()
@@ -202,16 +201,18 @@
             [total[:, :, :384], total[:, :, 384:]], axis=1
         ).astype(jnp.bfloat16)
 
-        def reply(r, carry):
-            e, t = source_of(r, dp, tk)
-            pltpu.make_async_remote_copy(
-                src_ref=back_send.at[r], dst_ref=back.at[mine],
-                send_sem=back_send_sem, recv_sem=back_sem.at[c],
-                device_id=(e, t), device_id_type=MESH,
-            ).start()
-            return carry
-
-        lax.fori_loop(jnp.where(c == 0, 1, c * PER), (c + 1) * PER, reply, 0)
+        for q, t in enumerate(tokens(c, -1)):
+            for p, e in enumerate(givers):
+                r = c * PER + q * 8 + p
+                away = pltpu.make_async_remote_copy(
+                    src_ref=back_send.at[r], dst_ref=back.at[mine],
+                    send_sem=back_send_sem, recv_sem=back_sem.at[c],
+                    device_id=(e, t), device_id_type=MESH,
+                )
+                if q + p:
+                    away.start()
+                else:
+                    pl.when(c > 0)(away.start)
 
         @pl.when(c == 0)
         def _():
@@ -224,8 +225,7 @@
     def finish(c, carry):
         span = pl.ds(c * PER, PER)
         pltpu.make_async_copy(back.at[span], back.at[span], back_sem.at[c]).wait()
-        for q in range(4):
-            t = ((tk // 4 + q) % 4) * 4 + (tk % 4 + c + 4 - q) % 4
+        for t in tokens(c, 1):
             answers = back[pl.ds(t * 8, 8)].reshape(128, 384)
             moe = lax.dot_general(
                 slots[t], answers, (((0,), (0,)), ((), ())), preferred_element_type=jnp.float32
@@ -236,7 +236,7 @@
 
     lax.fori_loop(0, CHUNKS, finish, 0)
     for k in range(1, 8):
-        pltpu.make_async_copy(ids_ref, ids_ref, id_send_sem.at[k - 1]).wait()
+        pltpu.make_async_copy(own_ids, own_ids, id_send_sem.at[k - 1]).wait()
         pltpu.make_async_copy(part_send.at[k], part_send.at[k], part_send_sem.at[k - 1]).wait()
     sent = pl.ds(1, CHUNKS * PER - 1)
     pltpu.make_async_copy(send.at[sent], send.at[sent], send_sem).wait()
@@ -259,6 +259,7 @@
             pltpu.VMEM((16, 128, 32), jnp.bfloat16),
             pltpu.VMEM((16, 16, 768), jnp.bfloat16),
             pltpu.VMEM(table.shape, jnp.bfloat16),
+            pltpu.VMEM((8, 256), jnp.int32),
             pltpu.VMEM((8, 8, 256), jnp.int32),
             pltpu.VMEM((384, table.shape[0]), jnp.bfloat16),
             pltpu.VMEM((384, 128), jnp.float32),
@@ -281,13 +282,10 @@
 
 
 def shards(dense_tokens, cold_table, cold_ids, routes, router, w_in, w_out):
-    ids = cold_ids.transpose(1, 0, 2).reshape(6, 256)
-    ids = jnp.concatenate([ids, ids[:2]], axis=0)
-    routes = routes.transpose(0, 2, 1)
     out = run_block(
         dense_tokens.transpose(1, 0, 2),
-        ids,
-        jnp.concatenate([routes, routes], axis=2),
+        cold_ids.transpose(1, 0, 2),
+        routes.transpose(0, 2, 1),
         router.transpose(0, 2, 1),
         cold_table,
         w_in[0, 0],

time: 98.1 us -> 77 us (0.78); the launches traced: 96.3 us -> 76.8 us
  Pallas kernels: 90.6 us -> 74.9 us
  other arithmetic: 2.09 us -> 0 us
  local copies, waits for them, and re-layouts: 3.55 us -> 1.86 us
    pallas_call x1, Pallas kernels: 90.6 us -> 74.9 us  [run_block(): pl.pallas_call(block_kernel, out_shape=jax.ShapeDtypeStruct((16, 16, 768)...]
    concatenate x2 -> x0, other arithmetic: 2.09 us -> none  [the longest x1 1.48 us: shards(): jnp.concatenate([routes, routes], axis=2)]
where the time goes in v2:
time: 77 us; the launch traced here: 76.8 us
  Pallas kernels  74.9 us (97%)
  local copies, waits for them, and re-layouts  1.86 us (2%)
    pallas_call x1, Pallas kernels, run_block(): pl.pallas_call(block_kernel, out_shape=jax.ShapeDtypeStruct((16, 16, 768)...  74.9 us
    transpose x1, local copies, waits for them, and re-layouts, shards(): return out.transpose(1, 0, 2)  1.86 us

profile of v2, /device:TPU:1, one launch (start us, length us, event | category | flops | bytes accessed | tf_op | source)
XLA Modules:
  0.0 76.8 jit_solution(9732030587884182872)
XLA Ops:
  0.0 74.9 %shard_map.73 = bf16[16,16,768]{2,1,0:T(8,128)(2,1)} custom-call(bf16[15,16,768]{2,1,0:T(8,128)(2,1)} %bitcast.10, s32[6,16,16]{2,1,0:T(8,128)} %bitcast.12, s32[16,2,16]{2,1,0:T(2,128)} %bitcast.13, bf16[16,8,768]{2,1,0:T(8,128)(2,1)} %bitcast.11, bf16[16384,128]{1,0:T(8,128)(2,1)} %table_hbm.1, bf16[768,3072]{1,0:T(8,128)(2,1)} %bitcast.8, ...), custom_call_target="tpu_custom_call" | custom-call | flops 9663676416 | bytes 9437184 | tf_op jit(solution)/shard_map/pallas_call | solution.py:248
  74.9 1.9 %copy.8 = bf16[16,16,768]{2,1,0:T(8,128)(2,1)} copy(bf16[16,16,768]{2,0,1:T(8,128)(2,1)} %bitcast.7) | data formatting | bytes 786432 | tf_op jit(solution)/shard_map/transpose | solution.py:294

commit v3 on v2

--- a/solution.py
+++ b/solution.py
@@ -71,6 +71,38 @@
         wide = jnp.concatenate([ids_ref[g]] * 16, axis=1)
         own_ids[g:g + 1, :] = jnp.sum(jnp.where(diagonal, wide, 0), axis=0, keepdims=True)
     own_ids[6:8, :] = jnp.zeros((2, 256), jnp.int32)
+    ids[0] = own_ids[...]
+    own_rows = table.shape[0]
+    low_row = lax.broadcasted_iota(jnp.int32, (256, 256), 0).astype(jnp.float32).astype(jnp.bfloat16)
+    one, none = jnp.ones((), jnp.bfloat16), jnp.zeros((), jnp.bfloat16)
+
+    def count(k):
+        for g in range(6):
+            local = ids[k, g:g + 1, :] - dp * own_rows
+            inside = (local >= 0) & (local < own_rows)
+            high = jnp.where(inside & diagonal, local // 256, -1)
+            high = high.astype(jnp.float32).astype(jnp.bfloat16)
+            low = jnp.where(inside, local % 256, 0).astype(jnp.float32).astype(jnp.bfloat16)
+            right = jnp.where(low_row == low, one, none).astype(jnp.float8_e4m3fn)
+            row = (k % 4) * 96 + g * 16
+            for v in range(own_rows // 4096):
+                lefts = jnp.concatenate(
+                    [jnp.where(high == float(v * 16 + i), one, none) for i in range(16)], axis=0
+                ).astype(jnp.float8_e4m3fn)
+                found = lax.dot_general(
+                    lefts, right, (((1,), (1,)), ((), ())), preferred_element_type=jnp.float32
+                ).astype(jnp.bfloat16)
+                for i in range(16):
+                    at = (v * 16 + i) * 256
+                    counts[row:row + 16, at:at + 256] = found[i * 16:(i + 1) * 16]
+
+    count(0)
+    pl.semaphore_wait(barrier, CHUNKS * PER - 1)
+    for k in range(1, 8):
+        pltpu.make_async_remote_copy(
+            src_ref=own_ids, dst_ref=ids.at[k], send_sem=id_send_sem.at[k - 1],
+            recv_sem=id_sem.at[k - 1], device_id=(peer_of(k, dp, 1), tk), device_id_type=MESH,
+        ).start()
     own_routes = jnp.concatenate([routes_ref[...]] * 2, axis=2)
     expert = lax.broadcasted_iota(jnp.int32, (16, 8, 32), 1)
     picks = (own_routes[:, 0:1, :] == expert) | (own_routes[:, 1:2, :] == expert)
@@ -90,46 +122,14 @@
             place[:, e:e + 1, :] == number, 1.0, 0.0
         ).astype(jnp.bfloat16)
 
-    pl.semaphore_wait(barrier, CHUNKS * PER - 1)
-    for k in range(1, 8):
-        pltpu.make_async_remote_copy(
-            src_ref=own_ids, dst_ref=ids.at[k], send_sem=id_send_sem.at[k - 1],
-            recv_sem=id_sem.at[k - 1], device_id=(peer_of(k, dp, 1), tk), device_id_type=MESH,
-        ).start()
-    ids[0] = own_ids[...]
-    load_table.wait()
-    own_rows = table.shape[0]
-    low_row = lax.broadcasted_iota(jnp.int32, (256, 256), 0).astype(jnp.float32).astype(jnp.bfloat16)
-    one, none = jnp.ones((), jnp.bfloat16), jnp.zeros((), jnp.bfloat16)
     for part_no in range(2):
         for k in range(part_no * 4, part_no * 4 + 4):
             if k:
                 pltpu.make_async_copy(ids.at[k], ids.at[k], id_sem.at[k - 1]).wait()
-
-        def count(step, carry):
-            for u in range(6):
-                group = step * 6 + u
-                local = ids[part_no * 4 + group // 6, pl.ds(group % 6, 1), :] - dp * own_rows
-                inside = (local >= 0) & (local < own_rows)
-                high = jnp.where(inside & diagonal, local // 256, -1)
-                high = high.astype(jnp.float32).astype(jnp.bfloat16)
-                low = jnp.where(inside, local % 256, 0).astype(jnp.float32).astype(jnp.bfloat16)
-                right = jnp.where(low_row == low, one, none)
-                rows = pl.ds(pl.multiple_of(group * 16, 16), 16)
-                for v in range(4):
-                    lefts = jnp.concatenate(
-                        [jnp.where(high == float(v * 16 + i), one, none) for i in range(16)], axis=0
-                    )
-                    found = lax.dot_general(
-                        lefts, right, (((1,), (1,)), ((), ())), preferred_element_type=jnp.float32
-                    ).astype(jnp.bfloat16)
-                    for i in range(16):
-                        at = (v * 16 + i) * 256
-                        counts[rows, at:at + 256] = found[i * 16:(i + 1) * 16]
-            return carry
-
-        lax.fori_loop(0, 24 // 6, count, 0)
+                count(k)
         sums[...] = jnp.zeros_like(sums)
+        if part_no == 0:
+            load_table.wait()
 
         def pool(step, carry):
             at = pl.ds(pl.multiple_of(step * 8192, 8192), 8192)
@@ -162,12 +162,12 @@
         rows = layer_norm(mixed.astype(jnp.float32) + features[h].astype(jnp.float32))
         rows = rows.astype(jnp.bfloat16)
         normed[h] = rows
-        halves = jnp.concatenate([rows[:, :384], rows[:, 384:]], axis=0)
-        out = jnp.dot(slots[h], halves, preferred_element_type=jnp.float32)
-        send[h * 8:(h + 1) * 8] = out.astype(jnp.bfloat16).reshape(8, 16, 384)
-
     for chunk in range(CHUNKS):
         for q, t in enumerate(tokens(chunk, 1)):
+            rows = normed[t]
+            halves = jnp.concatenate([rows[:, :384], rows[:, 384:]], axis=0)
+            out = jnp.dot(slots[t], halves, preferred_element_type=jnp.float32)
+            send[pl.ds(t * 8, 8)] = out.astype(jnp.bfloat16).reshape(8, 16, 384)
             for p, e in enumerate(experts):
                 r = chunk * PER + q * 8 + p
                 if r:

time: 77 us -> 71.8 us (0.932)
  Pallas kernels: 74.9 us -> 69.8 us
    pallas_call x1, Pallas kernels: 74.9 us -> 69.8 us  [run_block(): pl.pallas_call(block_kernel, out_shape=jax.ShapeDtypeStruct((16, 16, 768)...]
where the time goes in v3:
time: 71.8 us; the launch traced here: 71.7 us
  Pallas kernels  69.8 us (97%)
  local copies, waits for them, and re-layouts  1.86 us (3%)
    pallas_call x1, Pallas kernels, run_block(): pl.pallas_call(block_kernel, out_shape=jax.ShapeDtypeStruct((16, 16, 768)...  69.8 us
    transpose x1, local copies, waits for them, and re-layouts, shards(): return out.transpose(1, 0, 2)  1.86 us

profile of v3, /device:TPU:1, one launch (start us, length us, event | category | flops | bytes accessed | tf_op | source)
XLA Modules:
  0.0 71.7 jit_solution(10595158706518364850)
XLA Ops:
  0.0 69.8 %shard_map.73 = bf16[16,16,768]{2,1,0:T(8,128)(2,1)} custom-call(bf16[15,16,768]{2,1,0:T(8,128)(2,1)} %bitcast.10, s32[6,16,16]{2,1,0:T(8,128)} %bitcast.12, s32[16,2,16]{2,1,0:T(2,128)} %bitcast.13, bf16[16,8,768]{2,1,0:T(8,128)(2,1)} %bitcast.11, bf16[16384,128]{1,0:T(8,128)(2,1)} %table_hbm.1, bf16[768,3072]{1,0:T(8,128)(2,1)} %bitcast.8, ...), custom_call_target="tpu_custom_call" | custom-call | flops 9663676416 | bytes 9437184 | tf_op jit(solution)/shard_map/pallas_call | solution.py:248
  69.8 1.9 %copy.8 = bf16[16,16,768]{2,1,0:T(8,128)(2,1)} copy(bf16[16,16,768]{2,0,1:T(8,128)(2,1)} %bitcast.7) | data formatting | bytes 786432 | tf_op jit(solution)/shard_map/transpose | solution.py:294

commit v4 on v3

--- a/solution.py
+++ b/solution.py
@@ -11,6 +11,7 @@
 CHUNKS = 4
 PER = 32
 CAP = 8
+F8 = jnp.float8_e4m3fn
 MESH = pl.DeviceIdType.MESH
 
 
@@ -30,13 +31,21 @@
 
 
 def block_kernel(
-    dense_ref, ids_ref, routes_ref, router_ref, table_hbm, w1_hbm, w2_hbm, out_ref,
-    w1, w2, send, recv, back_send, back, slots, normed,
-    table, own_ids, ids, counts, sums, part_send, part,
+    dense_hbm, ids_hbm, routes_hbm, router_hbm, table_hbm, w1_hbm, w2_hbm, out_ref,
+    dense_ref, ids_ref, routes_ref, router_ref, w1, w2, send, recv, back_send, back, slots, normed,
+    table, pair, own_ids, ids, counts, sums, part_send, part,
     w_sem, send_sem, recv_sem, back_send_sem, back_sem, id_send_sem, id_sem, part_send_sem, part_sem,
 ):
     dp, tk = lax.axis_index("dp"), lax.axis_index("token")
     mine = tk * 8 + dp
+    load_ids = pltpu.make_async_copy(ids_hbm, ids_ref, w_sem.at[3])
+    load_routes = pltpu.make_async_copy(routes_hbm, routes_ref, w_sem.at[4])
+    load_dense = pltpu.make_async_copy(dense_hbm, dense_ref, w_sem.at[5])
+    load_router = pltpu.make_async_copy(router_hbm, router_ref, w_sem.at[6])
+    load_ids.start()
+    load_routes.start()
+    load_dense.start()
+    load_router.start()
     load_table = pltpu.make_async_copy(table_hbm, table, w_sem.at[2])
     load_table.start()
     load1 = pltpu.make_async_copy(w1_hbm, w1, w_sem.at[0])
@@ -67,6 +76,7 @@
                 if chunk + q + p:
                     pl.semaphore_signal(barrier, inc=1, device_id=(e, t), device_id_type=MESH)
 
+    load_ids.wait()
     for g in range(6):
         wide = jnp.concatenate([ids_ref[g]] * 16, axis=1)
         own_ids[g:g + 1, :] = jnp.sum(jnp.where(diagonal, wide, 0), axis=0, keepdims=True)
@@ -77,32 +87,49 @@
     one, none = jnp.ones((), jnp.bfloat16), jnp.zeros((), jnp.bfloat16)
 
     def count(k):
-        for g in range(6):
-            local = ids[k, g:g + 1, :] - dp * own_rows
-            inside = (local >= 0) & (local < own_rows)
-            high = jnp.where(inside & diagonal, local // 256, -1)
-            high = high.astype(jnp.float32).astype(jnp.bfloat16)
-            low = jnp.where(inside, local % 256, 0).astype(jnp.float32).astype(jnp.bfloat16)
-            right = jnp.where(low_row == low, one, none).astype(jnp.float8_e4m3fn)
+        for g in (0, 2, 4):
+            highs, rights = [], []
+            for i in range(2):
+                local = ids[k, g + i:g + i + 1, :] - dp * own_rows
+                inside = (local >= 0) & (local < own_rows)
+                high = jnp.where(inside & diagonal, local // 256, -1)
+                highs.append(high.astype(jnp.float32).astype(jnp.bfloat16))
+                low = jnp.where(inside, local % 256, 0).astype(jnp.float32).astype(jnp.bfloat16)
+                rights.append(jnp.where(low_row == low, one, none).astype(F8))
             row = (k % 4) * 96 + g * 16
             for v in range(own_rows // 4096):
-                lefts = jnp.concatenate(
-                    [jnp.where(high == float(v * 16 + i), one, none) for i in range(16)], axis=0
-                ).astype(jnp.float8_e4m3fn)
-                found = lax.dot_general(
-                    lefts, right, (((1,), (1,)), ((), ())), preferred_element_type=jnp.float32
-                ).astype(jnp.bfloat16)
+                found = []
+                for high, right in zip(highs, rights):
+                    lefts = jnp.concatenate(
+                        [jnp.where(high == float(v * 16 + i), one, none) for i in range(16)], axis=0
+                    ).astype(F8)
+                    found.append(lax.dot_general(
+                        lefts, right, (((1,), (1,)), ((), ())), preferred_element_type=jnp.float32
+                    ))
                 for i in range(16):
-                    at = (v * 16 + i) * 256
-                    counts[row:row + 16, at:at + 256] = found[i * 16:(i + 1) * 16]
+                    at, of = (v * 16 + i) * 256, slice(i * 16, (i + 1) * 16)
+                    counts[row:row + 32, at:at + 256] = jnp.concatenate(
+                        [found[0][of], found[1][of]], axis=0
+                    ).astype(F8)
+
+    def split(step, carry):
+        at = pl.ds(pl.multiple_of(step * 512, 512), 512)
+        rows = table[at, :].astype(jnp.float32) * 64.0
+        first = rows.astype(F8)
+        pair[at, :128] = first
+        pair[at, 128:] = ((rows - first.astype(jnp.float32)) * 16.0).astype(F8)
+        return carry
 
     count(0)
+    load_table.wait()
+    lax.fori_loop(0, own_rows // 512, split, 0)
     pl.semaphore_wait(barrier, CHUNKS * PER - 1)
     for k in range(1, 8):
         pltpu.make_async_remote_copy(
             src_ref=own_ids, dst_ref=ids.at[k], send_sem=id_send_sem.at[k - 1],
             recv_sem=id_sem.at[k - 1], device_id=(peer_of(k, dp, 1), tk), device_id_type=MESH,
         ).start()
+    load_routes.wait()
     own_routes = jnp.concatenate([routes_ref[...]] * 2, axis=2)
     expert = lax.broadcasted_iota(jnp.int32, (16, 8, 32), 1)
     picks = (own_routes[:, 0:1, :] == expert) | (own_routes[:, 1:2, :] == expert)
@@ -128,16 +155,14 @@
                 pltpu.make_async_copy(ids.at[k], ids.at[k], id_sem.at[k - 1]).wait()
                 count(k)
         sums[...] = jnp.zeros_like(sums)
-        if part_no == 0:
-            load_table.wait()
 
         def pool(step, carry):
             at = pl.ds(pl.multiple_of(step * 8192, 8192), 8192)
-            sums[...] += jnp.dot(counts[:, at], table[at, :], preferred_element_type=jnp.float32)
+            sums[...] += jnp.dot(counts[:, at], pair[at, :], preferred_element_type=jnp.float32)
             return carry
 
         lax.fori_loop(0, own_rows // 8192, pool, 0)
-        pooled = (sums[...] * 0.25).astype(jnp.bfloat16).reshape(4, 96, 128)
+        pooled = ((sums[:, :128] + sums[:, 128:] * (1.0 / 16.0)) * (0.25 / 64.0)).astype(jnp.bfloat16).reshape(4, 96, 128)
         for k in range(part_no * 4, part_no * 4 + 4):
             if k == 0:
                 part[0] = pooled[0]
@@ -156,6 +181,7 @@
     cold = cold.astype(jnp.bfloat16)
     cold = jnp.concatenate([cold[g * 16:(g + 1) * 16] for g in range(6)], axis=1)
 
+    load_dense.wait()
     features = [dense_ref[t] for t in range(15)] + [cold]
     for h in range(16):
         mixed = jnp.concatenate([f[:, h * 48:(h + 1) * 48] for f in features], axis=1)
@@ -179,6 +205,7 @@
     pltpu.make_async_copy(send.at[mine], recv.at[0], recv_sem.at[0]).start()
     load1.wait()
     load2.wait()
+    load_router.wait()
     which = lax.broadcasted_iota(jnp.int32, (PER * CAP, 8), 1) == dp
 
     def work(c, carry):
@@ -248,9 +275,13 @@
     return pl.pallas_call(
         block_kernel,
         out_shape=jax.ShapeDtypeStruct((16, 16, 768), jnp.bfloat16),
-        in_specs=[vmem] * 4 + [pl.BlockSpec(memory_space=pl.ANY)] * 3,
+        in_specs=[pl.BlockSpec(memory_space=pltpu.HBM)] * 7,
         out_specs=vmem,
         scratch_shapes=[
+            pltpu.VMEM(dense.shape, jnp.bfloat16),
+            pltpu.VMEM(ids.shape, jnp.int32),
+            pltpu.VMEM(routes.shape, jnp.int32),
+            pltpu.VMEM(router.shape, jnp.bfloat16),
             pltpu.VMEM((768, 3072), jnp.bfloat16),
             pltpu.VMEM((3072, 768), jnp.bfloat16),
         ]
@@ -259,13 +290,14 @@
             pltpu.VMEM((16, 128, 32), jnp.bfloat16),
             pltpu.VMEM((16, 16, 768), jnp.bfloat16),
             pltpu.VMEM(table.shape, jnp.bfloat16),
+            pltpu.VMEM((table.shape[0], 256), F8),
             pltpu.VMEM((8, 256), jnp.int32),
             pltpu.VMEM((8, 8, 256), jnp.int32),
-            pltpu.VMEM((384, table.shape[0]), jnp.bfloat16),
-            pltpu.VMEM((384, 128), jnp.float32),
+            pltpu.VMEM((384, table.shape[0]), F8),
+            pltpu.VMEM((384, 256), jnp.float32),
             pltpu.VMEM((8, 96, 128), jnp.bfloat16),
             pltpu.VMEM((8, 96, 128), jnp.bfloat16),
-            pltpu.SemaphoreType.DMA((3,)),
+            pltpu.SemaphoreType.DMA((7,)),
             pltpu.SemaphoreType.DMA,
             pltpu.SemaphoreType.DMA((CHUNKS,)),
             pltpu.SemaphoreType.DMA,

time: 71.8 us -> 68.2 us (0.950)
  Pallas kernels: 69.8 us -> 66.2 us
    pallas_call x1, Pallas kernels: 69.8 us -> 66.2 us  [run_block(): pl.pallas_call(block_kernel, out_shape=jax.ShapeDtypeStruct((16, 16, 768)...]
where the time goes in v4:
time: 68.2 us; the launch traced here: 68 us
  Pallas kernels  66.2 us (97%)
  local copies, waits for them, and re-layouts  1.86 us (3%)
    pallas_call x1, Pallas kernels, run_block(): pl.pallas_call(block_kernel, out_shape=jax.ShapeDtypeStruct((16, 16, 768)...  66.2 us
    transpose x1, local copies, waits for them, and re-layouts, shards(): return out.transpose(1, 0, 2)  1.86 us

profile of v4, /device:TPU:1, one launch (start us, length us, event | category | flops | bytes accessed | tf_op | source)
XLA Modules:
  0.0 68.0 jit_solution(511359034588031065)
XLA Ops:
  0.0 66.2 %shard_map.73 = bf16[16,16,768]{2,1,0:T(8,128)(2,1)} custom-call(bf16[15,16,768]{2,1,0:T(8,128)(2,1)} %bitcast.10, s32[6,16,16]{2,1,0:T(8,128)} %bitcast.12, s32[16,2,16]{2,1,0:T(2,128)} %bitcast.13, bf16[16,8,768]{2,1,0:T(8,128)(2,1)} %bitcast.11, bf16[16384,128]{1,0:T(8,128)(2,1)} %table_hbm.1, bf16[768,3072]{1,0:T(8,128)(2,1)} %bitcast.8, ...), custom_call_target="tpu_custom_call" | custom-call | flops 9663676416 | bytes 9437184 | tf_op jit(solution)/shard_map/pallas_call | solution.py:275
  66.2 1.9 %copy.8 = bf16[16,16,768]{2,1,0:T(8,128)(2,1)} copy(bf16[16,16,768]{2,0,1:T(8,128)(2,1)} %bitcast.7) | data formatting | bytes 786432 | tf_op jit(solution)/shard_map/transpose | solution.py:326

commit v5 on v4

--- a/solution.py
+++ b/solution.py
@@ -33,7 +33,7 @@
 def block_kernel(
     dense_hbm, ids_hbm, routes_hbm, router_hbm, table_hbm, w1_hbm, w2_hbm, out_ref,
     dense_ref, ids_ref, routes_ref, router_ref, w1, w2, send, recv, back_send, back, slots, normed,
-    table, pair, own_ids, ids, counts, sums, part_send, part,
+    table, pair, own_ids, ids, counts, sums, part_send, part, early,
     w_sem, send_sem, recv_sem, back_send_sem, back_sem, id_send_sem, id_sem, part_send_sem, part_sem,
 ):
     dp, tk = lax.axis_index("dp"), lax.axis_index("token")
@@ -173,6 +173,11 @@
                     recv_sem=part_sem.at[k - 1], device_id=(peer_of(k, dp, -1), tk),
                     device_id_type=MESH,
                 ).start()
+    load_dense.wait()
+    features = [dense_ref[t] for t in range(15)] + [jnp.zeros((16, 768), jnp.bfloat16)]
+    for h in range(16):
+        mixed = jnp.concatenate([f[:, h * 48:(h + 1) * 48] for f in features], axis=1)
+        early[h] = mixed.astype(jnp.float32) + features[h].astype(jnp.float32)
     for k in range(1, 8):
         pltpu.make_async_copy(part.at[k], part.at[k], part_sem.at[k - 1]).wait()
     cold = part[0].astype(jnp.float32)
@@ -181,12 +186,11 @@
     cold = cold.astype(jnp.bfloat16)
     cold = jnp.concatenate([cold[g * 16:(g + 1) * 16] for g in range(6)], axis=1)
 
-    load_dense.wait()
-    features = [dense_ref[t] for t in range(15)] + [cold]
+    gap = jnp.zeros((16, 720), jnp.bfloat16)
     for h in range(16):
-        mixed = jnp.concatenate([f[:, h * 48:(h + 1) * 48] for f in features], axis=1)
-        rows = layer_norm(mixed.astype(jnp.float32) + features[h].astype(jnp.float32))
-        rows = rows.astype(jnp.bfloat16)
+        late = jnp.concatenate([gap, cold[:, h * 48:(h + 1) * 48]], axis=1).astype(jnp.float32)
+        rows = early[h] + (late if h < 15 else late + cold.astype(jnp.float32))
+        rows = layer_norm(rows).astype(jnp.bfloat16)
         normed[h] = rows
     for chunk in range(CHUNKS):
         for q, t in enumerate(tokens(chunk, 1)):
@@ -194,7 +198,8 @@
             halves = jnp.concatenate([rows[:, :384], rows[:, 384:]], axis=0)
             out = jnp.dot(slots[t], halves, preferred_element_type=jnp.float32)
             send[pl.ds(t * 8, 8)] = out.astype(jnp.bfloat16).reshape(8, 16, 384)
-            for p, e in enumerate(experts):
+            for p in (4, 5, 2, 3, 6, 7, 0, 1):
+                e = experts[p]
                 r = chunk * PER + q * 8 + p
                 if r:
                     pltpu.make_async_remote_copy(
@@ -229,7 +234,8 @@
         ).astype(jnp.bfloat16)
 
         for q, t in enumerate(tokens(c, -1)):
-            for p, e in enumerate(givers):
+            for p in (4, 5, 2, 3, 6, 7, 0, 1):
+                e = givers[p]
                 r = c * PER + q * 8 + p
                 away = pltpu.make_async_remote_copy(
                     src_ref=back_send.at[r], dst_ref=back.at[mine],
@@ -297,6 +303,7 @@
             pltpu.VMEM((384, 256), jnp.float32),
             pltpu.VMEM((8, 96, 128), jnp.bfloat16),
             pltpu.VMEM((8, 96, 128), jnp.bfloat16),
+            pltpu.VMEM((16, 16, 768), jnp.float32),
             pltpu.SemaphoreType.DMA((7,)),
             pltpu.SemaphoreType.DMA,
             pltpu.SemaphoreType.DMA((CHUNKS,)),

time: 68.2 us -> 67.8 us (level)
  no operation moved by 1% of the time
where the time goes in v5:
time: 67.8 us; the launch traced here: 67.7 us
  Pallas kernels  65.8 us (97%)
  local copies, waits for them, and re-layouts  1.86 us (3%)
    pallas_call x1, Pallas kernels, run_block(): pl.pallas_call(block_kernel, out_shape=jax.ShapeDtypeStruct((16, 16, 768)...  65.8 us
    transpose x1, local copies, waits for them, and re-layouts, shards(): return out.transpose(1, 0, 2)  1.86 us

profile of v5, /device:TPU:1, one launch (start us, length us, event | category | flops | bytes accessed | tf_op | source)
XLA Modules:
  0.0 67.7 jit_solution(3249025540165331894)
XLA Ops:
  0.0 65.8 %shard_map.73 = bf16[16,16,768]{2,1,0:T(8,128)(2,1)} custom-call(bf16[15,16,768]{2,1,0:T(8,128)(2,1)} %bitcast.10, s32[6,16,16]{2,1,0:T(8,128)} %bitcast.12, s32[16,2,16]{2,1,0:T(2,128)} %bitcast.13, bf16[16,8,768]{2,1,0:T(8,128)(2,1)} %bitcast.11, bf16[16384,128]{1,0:T(8,128)(2,1)} %table_hbm.1, bf16[768,3072]{1,0:T(8,128)(2,1)} %bitcast.8, ...), custom_call_target="tpu_custom_call" | custom-call | flops 9663676416 | bytes 9437184 | tf_op jit(solution)/shard_map/pallas_call | solution.py:281
  65.8 1.9 %copy.8 = bf16[16,16,768]{2,1,0:T(8,128)(2,1)} copy(bf16[16,16,768]{2,0,1:T(8,128)(2,1)} %bitcast.7) | data formatting | bytes 786432 | tf_op jit(solution)/shard_map/transpose | solution.py:333
